TPU v7x, 512 devices: a whole 4x8x8 slice. The times are simulated.
512 devices in a mesh: tm: 32 (over x, z_hi, core), height: 16 (over z_lo, y).
Axes of the slice: x: 4, y: 8, z: 8 (z_hi: 4, z_lo: 2; z = z_hi * 2 + z_lo), core: 2. Of those that a mesh axis runs over, the one named last changes fastest.
Arguments:
- queries: bfloat16 [192, 128, 3, 1536], P('tm', 'height'), may hold values from -8 to 8
- keys: bfloat16 [192, 128, 3, 1536], P('tm', 'height'), may hold values from -8 to 8
- values: bfloat16 [192, 128, 3, 1536], P('tm', 'height'), may hold values from -6 to 6
- grad_out: bfloat16 [192, 128, 3, 1536], P('tm', 'height'), may hold values from -6 to 6
- window_radius: int32 [12, 2], replicated, may hold values from 0 to 1, as said below
- frames_valid: int32 [32], P('tm'), may hold values from 1 to 6, as said below
- rows_valid: int32 [16], P('height'), may hold values from 1 to 8, as said below
Outputs:
- grad_queries: bfloat16 [192, 128, 3, 1536], P('tm', 'height')
- grad_keys: bfloat16 [192, 128, 3, 1536], P('tm', 'height')
- grad_values: bfloat16 [192, 128, 3, 1536], P('tm', 'height')
Inputs may be any that keep to these rules, and one draw needn't show every extreme that they name: `window_radius`: some head reaches one tile along both frames and rows. `frames_valid`: some time tile has all 6 frames valid. `rows_valid`: some height tile has all 8 rows valid.
All inputs are finite; a program needn't handle non-finite values.
Results may differ from a plain program's by a relative error of at most 0.025.
Values may be sent and summed in bfloat16 or wider, within the bound.
A program may use at most 128 MiB of HBM per device.

v0:
```python
import jax
import jax.numpy as jnp
from jax import lax
from jax.sharding import PartitionSpec as P

HEADS = 12
HD = 128


masked_score = -1e30
heads_at_once = 4


def passed_along(block, axis, distance):
    devices = range(lax.axis_size(axis))
    route = [(i - distance, i) for i in devices if i - distance in devices]
    return lax.ppermute(block, axis, route)


def tile_masks(radius, frame_counts, row_counts, frames, rows, columns):
    frame_pos = jnp.arange(3 * frames, dtype=jnp.int32)
    row_pos = jnp.arange(3 * rows, dtype=jnp.int32)
    frame_tile = frame_pos // frames
    row_tile = row_pos // rows
    tile_slots = jnp.arange(3, dtype=jnp.int32)
    pick_frame = (frame_tile[:, None] == tile_slots[None, :]).astype(jnp.int32)
    pick_row = (row_tile[:, None] == tile_slots[None, :]).astype(jnp.int32)
    frame_limit = jnp.dot(jnp.dot(pick_frame, frame_counts), pick_row.T)
    row_limit = jnp.dot(jnp.dot(pick_frame, row_counts), pick_row.T)
    inside = ((frame_pos % frames)[:, None] < frame_limit) & ((row_pos % rows)[None, :] < row_limit)
    within_reach = (jnp.abs(frame_tile - 1)[None, :, None] <= radius[:, 0][:, None, None]) & (
        jnp.abs(row_tile - 1)[None, None, :] <= radius[:, 1][:, None, None]
    )
    flag_grid = within_reach & inside[None]
    return jnp.broadcast_to(flag_grid[..., None], flag_grid.shape + (columns,)).reshape(
        radius.shape[0], -1
    )


def both_counts(frame_line, row_line):
    frame_grid = frame_line[:, None] * (row_line[None, :] > 0).astype(jnp.int32)
    row_grid = row_line[None, :] * (frame_line[:, None] > 0).astype(jnp.int32)
    return (frame_grid, row_grid)


def clip_keep(tile_time, tile_row, time_span, row_span):
    offsets = jnp.arange(3, dtype=jnp.int32) - 1
    keep_time = ((tile_time + offsets) // time_span == tile_time // time_span).astype(jnp.int32)
    keep_row = ((tile_row + offsets) // row_span == tile_row // row_span).astype(jnp.int32)
    return (keep_time, keep_row)


def join_three(first_part, middle_part, last_part, axis_dim):
    return tuple(
        (
            jnp.concatenate([one_item, two_item, three_item], axis_dim)
            for one_item, two_item, three_item in zip(first_part, middle_part, last_part)
        )
    )


def summed_low(first_term, second_term, third_term):
    total = (
        first_term.astype(jnp.float32)
        + second_term.astype(jnp.float32)
        + third_term.astype(jnp.float32)
    )
    return total.astype(jnp.bfloat16)


def key_window_of(keys, values, frame_count, row_count):
    arrived = [passed_along((keys, values, frame_count), "tm", offset) for offset in (1, -1)]
    by_time = join_three(arrived[0], (keys, values, frame_count), arrived[1], 0)
    arrived = [
        passed_along((by_time[0], by_time[1], row_count), "height", offset) for offset in (1, -1)
    ]
    by_rows = join_three(arrived[0], (by_time[0], by_time[1], row_count), arrived[1], 0)
    block_pair = join_three(
        (arrived[0][0], arrived[0][1]), (by_time[0], by_time[1]), (arrived[1][0], arrived[1][1]), 1
    )
    frame_grid, row_grid = both_counts(by_time[2], by_rows[2])
    return (block_pair[0], block_pair[1], frame_grid, row_grid)


def return_partials(key_part, value_part):
    arrived = [
        passed_along((key_part[:, :, 1 + offset], value_part[:, :, 1 + offset]), "height", offset)
        for offset in (1, -1)
    ]
    band_key = summed_low(arrived[0][0], key_part[:, :, 1], arrived[1][0])
    band_value = summed_low(arrived[0][1], value_part[:, :, 1], arrived[1][1])
    arrived = [
        passed_along((band_key[1 + offset], band_value[1 + offset]), "tm", offset)
        for offset in (1, -1)
    ]
    return (
        summed_low(arrived[0][0], band_key[1], arrived[1][0]),
        summed_low(arrived[0][1], band_value[1], arrived[1][1]),
    )


def head_major(block):
    return block.reshape(block.shape[0], HEADS, HD).transpose(1, 0, 2)


def token_major(parts):
    joined = jnp.concatenate(parts, 0)
    return joined.transpose(1, 0, 2).reshape(joined.shape[1], HEADS * HD)


def attend_tile(query, key_window, value_window, grad, key_allowed):
    score_scale = HD ** (-0.5)
    query_heads = head_major(query)
    key_heads = head_major(key_window)
    value_heads = head_major(value_window)
    grad_heads = head_major(grad)
    query_parts = []
    key_parts = []
    value_parts = []
    for group_index in range(HEADS // heads_at_once):
        head_lo = group_index * heads_at_once
        head_hi = head_lo + heads_at_once
        query_group = query_heads[head_lo:head_hi]
        key_group = key_heads[head_lo:head_hi]
        value_group = value_heads[head_lo:head_hi]
        grad_group = grad_heads[head_lo:head_hi]
        allowed = key_allowed[head_lo:head_hi][:, None, :]
        scores = (
            jnp.einsum("hqd,hkd->hqk", query_group, key_group, preferred_element_type=jnp.float32)
            * score_scale
        )
        scores = jnp.where(allowed, scores, masked_score)
        row_max = jnp.max(scores, axis=2, keepdims=True)
        raised = jnp.exp(scores - row_max)
        totals = jnp.sum(raised, axis=2, keepdims=True)
        weights = raised / totals
        weights_low = weights.astype(jnp.bfloat16)
        output = jnp.einsum(
            "hqk,hkd->hqd", weights_low, value_group, preferred_element_type=jnp.float32
        ).astype(jnp.bfloat16)
        row_delta = jnp.einsum(
            "hqd,hqd->hq", grad_group, output, preferred_element_type=jnp.float32
        )
        grad_weights = jnp.einsum(
            "hqd,hkd->hqk", grad_group, value_group, preferred_element_type=jnp.float32
        )
        grad_low = (weights * (grad_weights - row_delta[:, :, None])).astype(jnp.bfloat16)
        grad_query = (
            jnp.einsum("hqk,hkd->hqd", grad_low, key_group, preferred_element_type=jnp.float32)
            * score_scale
        )
        grad_key = (
            jnp.einsum("hqk,hqd->hkd", grad_low, query_group, preferred_element_type=jnp.float32)
            * score_scale
        )
        grad_value = jnp.einsum(
            "hqk,hqd->hkd", weights_low, grad_group, preferred_element_type=jnp.float32
        )
        query_parts.append(grad_query.astype(jnp.bfloat16))
        key_parts.append(grad_key.astype(jnp.bfloat16))
        value_parts.append(grad_value.astype(jnp.bfloat16))
    return (token_major(query_parts), token_major(key_parts), token_major(value_parts))


def on_device(queries, keys, values, grad_out, window_radius, frames_valid, rows_valid):
    frames, rows, columns, width = queries.shape
    query_count = frames * rows * columns
    key_block, value_block, frame_grid, row_grid = key_window_of(
        keys, values, frames_valid, rows_valid
    )
    keep_time, keep_row = clip_keep(
        lax.axis_index("tm"), lax.axis_index("height"), lax.axis_size("tm"), lax.axis_size("height")
    )
    clip_grid = keep_time[:, None] * keep_row[None, :]
    frame_grid = frame_grid * clip_grid
    row_grid = row_grid * clip_grid
    key_allowed = tile_masks(window_radius, frame_grid, row_grid, frames, rows, columns)
    grad_query, key_part, value_part = attend_tile(
        queries.reshape(query_count, width),
        key_block.reshape(-1, width),
        value_block.reshape(-1, width),
        grad_out.reshape(query_count, width),
        key_allowed,
    )
    key_part = key_part.reshape(3, frames, 3, rows, columns, width)
    value_part = value_part.reshape(3, frames, 3, rows, columns, width)
    grad_keys, grad_values = return_partials(key_part, value_part)
    return (grad_query.reshape(queries.shape), grad_keys, grad_values)


def solution(mesh):
    placed = (
        P("tm", "height", None, None),
        P("tm", "height", None, None),
        P("tm", "height", None, None),
        P("tm", "height", None, None),
        P(),
        P("tm"),
        P("height"),
    )
    return jax.shard_map(
        on_device,
        mesh=mesh,
        in_specs=placed,
        out_specs=(
            P("tm", "height", None, None),
            P("tm", "height", None, None),
            P("tm", "height", None, None),
        ),
        check_vma=False,
    )
```

profile of v0, /device:TPU:382, one launch (start us, length us, event | category | flops | bytes accessed | tf_op | source)
XLA Modules:
  0.0 374.7 jit_solution(12652351661158782022)
XLA Ops:
  2.7 5.8 %collective-permute-start.1 = (s32[1]{0:T(128)}, s32[1]{0:T(128)}, u32[]{:S(2)}, u32[]{:S(2)}) collective-permute-start(s32[1]{0:T(128)} %param.12), channel_id=1, source_target_pairs={{16,0},{32,16},{48,32},{64,48},{80,64},{96,80},{112,96},{128,112},... | collective-permute-start | bytes 20 | tf_op jit(solution)/shard_map/ppermute | solution.py:17
  9.8 5.1 %collective-permute-start.3 = (s32[1]{0:T(128)}, s32[1]{0:T(128)}, u32[]{:S(2)}, u32[]{:S(2)}) collective-permute-start(s32[1]{0:T(128)} %param.13), channel_id=1, source_target_pairs={{1,0},{2,1},{3,2},{4,3},{5,4},{6,5},{7,6},{8,7},{9,8},{10,9},{11,1... | collective-permute-start | bytes 20 | tf_op jit(solution)/shard_map/ppermute | solution.py:17
  23.6 5.8 %collective-permute-start.5 = (bf16[6,8,3,1536]{3,1,2,0:T(8,128)(2,1)S(1)}, bf16[6,8,3,1536]{3,1,2,0:T(8,128)(2,1)S(1)}, u32[]{:S(2)}, u32[]{:S(2)}) collective-permute-start(bf16[6,8,3,1536]{3,1,2,0:T(8,128)(2,1)S(1)} %copy-done.17), channel_id=1, source_target_pairs={{16,0},{32,16},{48,32},{64,48},{80,64},{96,80},{112,96},{128,112},... | collective-permute-start | bytes 1327112 | tf_op jit(solution)/shard_map/ppermute | solution.py:17
  32.6 5.7 %collective-permute-start.9 = (bf16[6,8,3,1536]{3,1,2,0:T(8,128)(2,1)S(1)}, bf16[6,8,3,1536]{3,1,2,0:T(8,128)(2,1)S(1)}, u32[]{:S(2)}, u32[]{:S(2)}) collective-permute-start(bf16[6,8,3,1536]{3,1,2,0:T(8,128)(2,1)S(1)} %copy-done.18), channel_id=1, source_target_pairs={{16,0},{32,16},{48,32},{64,48},{80,64},{96,80},{112,96},{128,112},... | collective-permute-start | bytes 1327112 | tf_op jit(solution)/shard_map/ppermute | solution.py:17
  38.4 61.6 %collective-permute-done.5 = bf16[6,8,3,1536]{3,1,2,0:T(8,128)(2,1)S(1)} collective-permute-done((bf16[6,8,3,1536]{3,1,2,0:T(8,128)(2,1)S(1)}, bf16[6,8,3,1536]{3,1,2,0:T(8,128)(2,1)S(1)}, u32[]{:S(2)}, u32[]{:S(2)}) %collective-permute-start.5) | collective-permute-done | bytes 442400 | tf_op jit(solution)/shard_map/ppermute | solution.py:17
  104.8 4.7 %collective-permute-start.11 = (bf16[18,8,3,1536]{3,1,2,0:T(8,128)(2,1)S(1)}, bf16[18,8,3,1536]{3,1,2,0:T(8,128)(2,1)}, u32[]{:S(2)}, u32[]{:S(2)}) collective-permute-start(bf16[18,8,3,1536]{3,1,2,0:T(8,128)(2,1)S(1)} %constant_dynamic-update-slice_fusion.3), channel_id=1, source_target_pairs={{1,0},{2,1},{3,2},{4,3},{5,4},{6,5},{7,6},{8,7},{9,8},{10,9},{11,1... | collective-permute-start | bytes 3981320 | tf_op jit(solution)/shard_map/ppermute | solution.py:17
  115.6 14.2 %collective-permute-done.7 = bf16[18,8,3,1536]{3,1,2,0:T(8,128)(2,1)} collective-permute-done((bf16[18,8,3,1536]{3,1,2,0:T(8,128)(2,1)S(1)}, bf16[18,8,3,1536]{3,1,2,0:T(8,128)(2,1)}, u32[]{:S(2)}, u32[]{:S(2)}) %collective-permute-start.7) | collective-permute-done | bytes 1327136 | tf_op jit(solution)/shard_map/ppermute | solution.py:17
  129.8 5.9 %collective-permute-done.6 = bf16[18,8,3,1536]{3,1,2,0:T(8,128)(2,1)} collective-permute-done((bf16[18,8,3,1536]{3,1,2,0:T(8,128)(2,1)S(1)}, bf16[18,8,3,1536]{3,1,2,0:T(8,128)(2,1)}, u32[]{:S(2)}, u32[]{:S(2)}) %collective-permute-start.6) | collective-permute-done | bytes 1327136 | tf_op jit(solution)/shard_map/ppermute | solution.py:17
  137.5 5.1 %copy.28 = bf16[18,24,3,1536]{3,2,1,0:T(4,128)(2,1)} copy(bf16[18,24,3,1536]{3,1,2,0:T(8,128)(2,1)S(1)} %pad_maximum_fusion) | data formatting | bytes 7962624 | tf_op jit(solution)/shard_map/concatenate | solution.py:56
  142.6 12.5 %reshape_reshape.21 = bf16[1296,12,128]{2,1,0:T(8,128)(2,1)} reshape(bf16[18,24,3,1536]{3,2,1,0:T(4,128)(2,1)} %copy.28) | data formatting | bytes 7962624 | tf_op jit(solution)/shard_map/reshape;reshape | solution.py:103
  155.1 5.4 %copy.86 = bf16[1296,12,128]{2,0,1:T(8,128)(2,1)} copy(bf16[1296,12,128]{2,1,0:T(8,128)(2,1)} %reshape_reshape.21) | data formatting | bytes 7962624 | tf_op jit(solution)/shard_map/reshape;reshape | solution.py:103
  160.5 3.6 collective-permute-done.10
  166.0 5.1 %copy.32 = bf16[18,24,3,1536]{3,2,1,0:T(4,128)(2,1)} copy(bf16[18,24,3,1536]{3,1,2,0:T(8,128)(2,1)S(1)} %pad_maximum_fusion.1) | data formatting | bytes 7962624 | tf_op jit(solution)/shard_map/concatenate | solution.py:56
  171.1 12.6 %reshape_reshape.23 = bf16[1296,12,128]{2,1,0:T(8,128)(2,1)} reshape(bf16[18,24,3,1536]{3,2,1,0:T(4,128)(2,1)} %copy.32) | data formatting | bytes 7962624 | tf_op jit(solution)/shard_map/reshape;reshape | solution.py:103
  183.8 5.6 %copy.85 = bf16[1296,12,128]{2,0,1:T(8,128)(2,1)} copy(bf16[1296,12,128]{2,1,0:T(8,128)(2,1)} %reshape_reshape.23) | data formatting | bytes 7962624 | tf_op jit(solution)/shard_map/reshape;reshape | solution.py:103
  193.4 6.1 %convolution_convert_fusion.2 = bf16[4,1296,128]{2,1,0:T(8,128)(2,1)} fusion(bf16[12,144,128]{2,1,0:T(8,128)(2,1)} %bitcast.135, f32[4,144]{1,0:T(4,128)S(1)} %get-tuple-element.30, f32[4,144,1296]{2,1,0:T(8,128)} %copy-done.2), kind=kOutput, calls=%fused_computation.47 | convolution fusion | flops 194007888 | bytes 7964928 | tf_op jit(solution)/shard_map/hqk,hqd->hkd/dot_general | solution.py:156
  199.5 4.7 %fusion.101 = f32[4,144]{1,0:T(4,128)S(1)} fusion(bf16[12,1296,128]{2,1,0:T(8,128)(2,1)} %bitcast.123, bf16[12,144,128]{2,1,0:T(8,128)(2,1)} %bitcast.136, f32[4,144]{1,0:T(4,128)S(1)} %get-tuple-element.30, f32[4,144,1296]{2,1,0:T(8,128)} %copy-done.2), kind=kOutput, calls=%fused_computation.98 | convolution fusion | flops 193712400 | bytes 7967232 | tf_op jit(solution)/shard_map/hqk,hkd->hqd/dot_general | solution.py:138
  209.2 4.2 %convolution_convert_fusion.1 = bf16[4,1296,128]{2,1,0:T(8,128)(2,1)} fusion(bf16[12,144,128]{2,1,0:T(8,128)(2,1)} %bitcast.138, f32[4,144]{1,0:T(4,128)S(1)} %get-tuple-element.28, f32[4,144,1296]{2,1,0:T(8,128)S(1)} %fusion.16), kind=kOutput, calls=%fused_computation.46 | convolution fusion | flops 194007888 | bytes 7966720 | tf_op jit(solution)/shard_map/hqk,hqd->hkd/dot_general | solution.py:156
  220.8 4.1 %convolution_convert_fusion = bf16[4,1296,128]{2,1,0:T(8,128)(2,1)} fusion(bf16[12,144,128]{2,1,0:T(8,128)(2,1)} %bitcast.140, f32[4,144]{1,0:T(4,128)S(1)} %get-tuple-element.26, f32[4,144,1296]{2,1,0:T(8,128)S(1)} %fusion.19), kind=kOutput, calls=%fused_computation.45 | convolution fusion | flops 194007888 | bytes 7966720 | tf_op jit(solution)/shard_map/hqk,hqd->hkd/dot_general | solution.py:156
  237.4 10.0 %copy.46 = bf16[1296,12,128]{2,1,0:T(8,128)(2,1)} copy(bf16[1296,12,128]{2,0,1:T(8,128)(2,1)S(1)} %maximum_bitcast_fusion.1) | data formatting | bytes 7962624 | tf_op jit(solution)/shard_map/transpose | solution.py:108
  247.4 11.9 %reshape_reshape.27 = bf16[3,6,3,8,3,1536]{5,4,3,2,1,0:T(4,128)(2,1)} reshape(bf16[1296,12,128]{2,1,0:T(8,128)(2,1)} %copy.46) | data formatting | bytes 7962624 | tf_op jit(solution)/shard_map/reshape;reshape | solution.py:186
  261.0 9.7 %copy.37 = bf16[1296,12,128]{2,1,0:T(8,128)(2,1)} copy(bf16[1296,12,128]{2,0,1:T(8,128)(2,1)S(1)} %maximum_bitcast_fusion) | data formatting | bytes 7962624 | tf_op jit(solution)/shard_map/transpose | solution.py:108
  270.7 12.2 %reshape_reshape.26 = bf16[3,6,3,8,3,1536]{5,4,3,2,1,0:T(4,128)(2,1)} reshape(bf16[1296,12,128]{2,1,0:T(8,128)(2,1)} %copy.37) | data formatting | bytes 7962624 | tf_op jit(solution)/shard_map/reshape;reshape | solution.py:185
  283.0 3.7 slice_bitcast_fusion.5
  297.1 5.9 %collective-permute-start.17 = (bf16[3,6,8,3,1536]{4,2,3,1,0:T(8,128)(2,1)}, bf16[3,6,8,3,1536]{4,2,3,1,0:T(8,128)(2,1)}, u32[]{:S(2)}, u32[]{:S(2)}) collective-permute-start(bf16[3,6,8,3,1536]{4,2,3,1,0:T(8,128)(2,1)} %copy.49), channel_id=1, source_target_pairs={{1,0},{2,1},{3,2},{4,3},{5,4},{6,5},{7,6},{8,7},{9,8},{10,9},{11,1... | collective-permute-start | bytes 3981320 | tf_op jit(solution)/shard_map/ppermute | solution.py:17
  307.5 13.1 %collective-permute-done.13 = bf16[3,6,8,3,1536]{4,2,3,1,0:T(8,128)(2,1)} collective-permute-done((bf16[3,6,8,3,1536]{4,2,3,1,0:T(8,128)(2,1)}, bf16[3,6,8,3,1536]{4,2,3,1,0:T(8,128)(2,1)}, u32[]{:S(2)}, u32[]{:S(2)}) %collective-permute-start.13) | collective-permute-done | bytes 1327136 | tf_op jit(solution)/shard_map/ppermute | solution.py:17
  320.6 5.4 %collective-permute-done.12 = bf16[3,6,8,3,1536]{4,2,3,1,0:T(8,128)(2,1)} collective-permute-done((bf16[3,6,8,3,1536]{4,2,3,1,0:T(8,128)(2,1)}, bf16[3,6,8,3,1536]{4,2,3,1,0:T(8,128)(2,1)}, u32[]{:S(2)}, u32[]{:S(2)}) %collective-permute-start.12) | collective-permute-done | bytes 1327136 | tf_op jit(solution)/shard_map/ppermute | solution.py:17
  326.1 4.4 %fusion.12 = bf16[3,6,8,3,1536]{4,3,2,1,0:T(4,128)(2,1)S(1)} fusion(bf16[3,6,3,8,3,1536]{5,4,3,2,1,0:T(4,128)(2,1)} %reshape_reshape.26, bf16[3,6,8,3,1536]{4,2,3,1,0:T(8,128)(2,1)} %collective-permute-done.13, bf16[3,6,8,3,1536]{4,2,3,1,0:T(8,128)(2,1)} %collective-permute-done.12), kind=kLoop, calls=%fused_computation.26 | loop fusion | flops 3981312 | bytes 5308416 | tf_op jit(solution)/shard_map/convert_element_type | solution.py:68
  335.5 13.6 %collective-permute-done.17 = bf16[3,6,8,3,1536]{4,2,3,1,0:T(8,128)(2,1)} collective-permute-done((bf16[3,6,8,3,1536]{4,2,3,1,0:T(8,128)(2,1)}, bf16[3,6,8,3,1536]{4,2,3,1,0:T(8,128)(2,1)}, u32[]{:S(2)}, u32[]{:S(2)}) %collective-permute-start.17) | collective-permute-done | bytes 1327136 | tf_op jit(solution)/shard_map/ppermute | solution.py:17
  349.0 5.2 %collective-permute-done.16 = bf16[3,6,8,3,1536]{4,2,3,1,0:T(8,128)(2,1)} collective-permute-done((bf16[3,6,8,3,1536]{4,2,3,1,0:T(8,128)(2,1)S(1)}, bf16[3,6,8,3,1536]{4,2,3,1,0:T(8,128)(2,1)}, u32[]{:S(2)}, u32[]{:S(2)}) %collective-permute-start.16) | collective-permute-done | bytes 1327136 | tf_op jit(solution)/shard_map/ppermute | solution.py:17
  354.2 4.4 %fusion.10 = bf16[3,6,8,3,1536]{4,3,2,1,0:T(4,128)(2,1)S(1)} fusion(bf16[3,6,3,8,3,1536]{5,4,3,2,1,0:T(4,128)(2,1)} %reshape_reshape.27, bf16[3,6,8,3,1536]{4,2,3,1,0:T(8,128)(2,1)} %collective-permute-done.17, bf16[3,6,8,3,1536]{4,2,3,1,0:T(8,128)(2,1)} %collective-permute-done.16), kind=kLoop, calls=%fused_computation.23 | loop fusion | flops 3981312 | bytes 5308416 | tf_op jit(solution)/shard_map/convert_element_type | solution.py:68
  367.0 5.9 %collective-permute-done.18 = bf16[6,8,3,1536]{3,1,2,0:T(8,128)(2,1)S(1)} collective-permute-done((bf16[6,8,3,1536]{3,1,2,0:T(8,128)(2,1)S(1)}, bf16[6,8,3,1536]{3,1,2,0:T(8,128)(2,1)S(1)}, u32[]{:S(2)}, u32[]{:S(2)}) %collective-permute-start.18) | collective-permute-done | bytes 442400 | tf_op jit(solution)/shard_map/ppermute | solution.py:17
  (144 shorter events, 88.6 us)
Async XLA Ops:
  0.6 21.0 %copy-start.19 = (bf16[6,8,3,1536]{3,1,2,0:T(8,128)(2,1)S(1)}, bf16[6,8,3,1536]{3,1,2,0:T(8,128)(2,1)}, u32[]{:S(2)}) copy-start(bf16[6,8,3,1536]{3,1,2,0:T(8,128)(2,1)} %param.10) | copy-start | bytes 1327108
  0.6 22.9 %collective-permute-start = (s32[1]{0:T(128)}, s32[1]{0:T(128)}, u32[]{:S(2)}, u32[]{:S(2)}) collective-permute-start(s32[1]{0:T(128)} %param.12), channel_id=1, source_target_pairs={{0,16},{16,32},{32,48},{48,64},{64,80},{80,96},{96,112},{112,128},... | collective-permute-start | bytes 20 | tf_op jit(solution)/shard_map/ppermute | solution.py:17
  2.7 26.6 %collective-permute-start.1 = (s32[1]{0:T(128)}, s32[1]{0:T(128)}, u32[]{:S(2)}, u32[]{:S(2)}) collective-permute-start(s32[1]{0:T(128)} %param.12), channel_id=1, source_target_pairs={{16,0},{32,16},{48,32},{64,48},{80,64},{96,80},{112,96},{128,112},... | collective-permute-start | bytes 20 | tf_op jit(solution)/shard_map/ppermute | solution.py:17
  8.5 101.1 %collective-permute-start.2 = (s32[1]{0:T(128)}, s32[1]{0:T(128)}, u32[]{:S(2)}, u32[]{:S(2)}) collective-permute-start(s32[1]{0:T(128)} %param.13), channel_id=1, source_target_pairs={{0,1},{1,2},{2,3},{3,4},{4,5},{5,6},{6,7},{7,8},{8,9},{9,10},{10,1... | collective-permute-start | bytes 20 | tf_op jit(solution)/shard_map/ppermute | solution.py:17
  9.8 101.2 %collective-permute-start.3 = (s32[1]{0:T(128)}, s32[1]{0:T(128)}, u32[]{:S(2)}, u32[]{:S(2)}) collective-permute-start(s32[1]{0:T(128)} %param.13), channel_id=1, source_target_pairs={{1,0},{2,1},{3,2},{4,3},{5,4},{6,5},{7,6},{8,7},{9,8},{10,9},{11,1... | collective-permute-start | bytes 20 | tf_op jit(solution)/shard_map/ppermute | solution.py:17
  14.8 17.8 %collective-permute-start.4 = (bf16[6,8,3,1536]{3,1,2,0:T(8,128)(2,1)}, bf16[6,8,3,1536]{3,1,2,0:T(8,128)(2,1)S(1)}, u32[]{:S(2)}, u32[]{:S(2)}) collective-permute-start(bf16[6,8,3,1536]{3,1,2,0:T(8,128)(2,1)} %param.8), channel_id=1, source_target_pairs={{0,16},{16,32},{32,48},{48,64},{64,80},{80,96},{96,112},{112,128},... | collective-permute-start | bytes 1327112 | tf_op jit(solution)/shard_map/ppermute | solution.py:17
  18.9 10.5 %copy-start.18 = (bf16[6,8,3,1536]{3,1,2,0:T(8,128)(2,1)S(1)}, bf16[6,8,3,1536]{3,1,2,0:T(8,128)(2,1)}, u32[]{:S(2)}) copy-start(bf16[6,8,3,1536]{3,1,2,0:T(8,128)(2,1)} %param.9) | copy-start | bytes 1327108
  23.6 76.5 %collective-permute-start.5 = (bf16[6,8,3,1536]{3,1,2,0:T(8,128)(2,1)S(1)}, bf16[6,8,3,1536]{3,1,2,0:T(8,128)(2,1)S(1)}, u32[]{:S(2)}, u32[]{:S(2)}) collective-permute-start(bf16[6,8,3,1536]{3,1,2,0:T(8,128)(2,1)S(1)} %copy-done.17), channel_id=1, source_target_pairs={{16,0},{32,16},{48,32},{64,48},{80,64},{96,80},{112,96},{128,112},... | collective-permute-start | bytes 1327112 | tf_op jit(solution)/shard_map/ppermute | solution.py:17
  29.3 73.1 %collective-permute-start.8 = (bf16[6,8,3,1536]{3,1,2,0:T(8,128)(2,1)S(1)}, bf16[6,8,3,1536]{3,1,2,0:T(8,128)(2,1)S(1)}, u32[]{:S(2)}, u32[]{:S(2)}) collective-permute-start(bf16[6,8,3,1536]{3,1,2,0:T(8,128)(2,1)S(1)} %copy-done.18), channel_id=1, source_target_pairs={{0,16},{16,32},{32,48},{48,64},{64,80},{80,96},{96,112},{112,128},... | collective-permute-start | bytes 1327112 | tf_op jit(solution)/shard_map/ppermute | solution.py:17
  32.6 72.2 %collective-permute-start.9 = (bf16[6,8,3,1536]{3,1,2,0:T(8,128)(2,1)S(1)}, bf16[6,8,3,1536]{3,1,2,0:T(8,128)(2,1)S(1)}, u32[]{:S(2)}, u32[]{:S(2)}) collective-permute-start(bf16[6,8,3,1536]{3,1,2,0:T(8,128)(2,1)S(1)} %copy-done.18), channel_id=1, source_target_pairs={{16,0},{32,16},{48,32},{64,48},{80,64},{96,80},{112,96},{128,112},... | collective-permute-start | bytes 1327112 | tf_op jit(solution)/shard_map/ppermute | solution.py:17
  100.1 29.7 %collective-permute-start.7 = (bf16[18,8,3,1536]{3,1,2,0:T(8,128)(2,1)S(1)}, bf16[18,8,3,1536]{3,1,2,0:T(8,128)(2,1)}, u32[]{:S(2)}, u32[]{:S(2)}) collective-permute-start(bf16[18,8,3,1536]{3,1,2,0:T(8,128)(2,1)S(1)} %constant_dynamic-update-slice_fusion), channel_id=1, source_target_pairs={{1,0},{2,1},{3,2},{4,3},{5,4},{6,5},{7,6},{8,7},{9,8},{10,9},{11,1... | collective-permute-start | bytes 3981320 | tf_op jit(solution)/shard_map/ppermute | solution.py:17
  102.5 33.2 %collective-permute-start.6 = (bf16[18,8,3,1536]{3,1,2,0:T(8,128)(2,1)S(1)}, bf16[18,8,3,1536]{3,1,2,0:T(8,128)(2,1)}, u32[]{:S(2)}, u32[]{:S(2)}) collective-permute-start(bf16[18,8,3,1536]{3,1,2,0:T(8,128)(2,1)S(1)} %constant_dynamic-update-slice_fusion), channel_id=1, source_target_pairs={{0,1},{1,2},{2,3},{3,4},{4,5},{5,6},{6,7},{7,8},{8,9},{9,10},{10,1... | collective-permute-start | bytes 3981320 | tf_op jit(solution)/shard_map/ppermute | solution.py:17
  104.8 55.7 %collective-permute-start.11 = (bf16[18,8,3,1536]{3,1,2,0:T(8,128)(2,1)S(1)}, bf16[18,8,3,1536]{3,1,2,0:T(8,128)(2,1)}, u32[]{:S(2)}, u32[]{:S(2)}) collective-permute-start(bf16[18,8,3,1536]{3,1,2,0:T(8,128)(2,1)S(1)} %constant_dynamic-update-slice_fusion.3), channel_id=1, source_target_pairs={{1,0},{2,1},{3,2},{4,3},{5,4},{6,5},{7,6},{8,7},{9,8},{10,9},{11,1... | collective-permute-start | bytes 3981320 | tf_op jit(solution)/shard_map/ppermute | solution.py:17
  109.5 54.6 %collective-permute-start.10 = (bf16[18,8,3,1536]{3,1,2,0:T(8,128)(2,1)S(1)}, bf16[18,8,3,1536]{3,1,2,0:T(8,128)(2,1)}, u32[]{:S(2)}, u32[]{:S(2)}) collective-permute-start(bf16[18,8,3,1536]{3,1,2,0:T(8,128)(2,1)S(1)} %constant_dynamic-update-slice_fusion.3), channel_id=1, source_target_pairs={{0,1},{1,2},{2,3},{3,4},{4,5},{5,6},{6,7},{7,8},{8,9},{9,10},{10,1... | collective-permute-start | bytes 3981320 | tf_op jit(solution)/shard_map/ppermute | solution.py:17
  183.7 5.6 %copy-start = (bf16[1296,12,128]{2,0,1:T(8,128)(2,1)S(1)}, bf16[1296,12,128]{2,0,1:T(8,128)(2,1)}, u32[]{:S(2)}) copy-start(bf16[1296,12,128]{2,0,1:T(8,128)(2,1)} %copy.86) | copy-start | bytes 11943940
  183.7 5.6 %copy-start.4 = (bf16[144,12,128]{2,0,1:T(8,128)(2,1)S(1)}, bf16[144,12,128]{2,0,1:T(8,128)(2,1)}, u32[]{:S(2)}) copy-start(bf16[144,12,128]{2,0,1:T(8,128)(2,1)} %copy.88) | copy-start | bytes 1327108
  224.9 5.3 %copy-start.6 = (f32[4,144,1296]{2,1,0:T(8,128)S(1)}, f32[4,144,1296]{2,1,0:T(8,128)}, u32[]{:S(2)}) copy-start(f32[4,144,1296]{2,1,0:T(8,128)} %get-tuple-element.29) | copy-start | bytes 8957956
  224.9 5.3 %copy-start.20 = (bf16[144,12,128]{2,0,1:T(8,128)(2,1)S(1)}, bf16[144,12,128]{2,0,1:T(8,128)(2,1)}, u32[]{:S(2)}) copy-start(bf16[144,12,128]{2,0,1:T(8,128)(2,1)} %copy.87) | copy-start | bytes 1327108
  270.7 22.4 %slice-start = ((s8[5308416]{0:T(1024)(128)(4,1)}), s8[1114112]{0:T(1024)(128)(4,1)S(1)}, s32[]{:S(2)}) async-start(s8[5308416]{0:T(1024)(128)(4,1)} %bitcast.121), calls=%async_computation | async-start | bytes 2228224
  283.0 10.2 %slice-start.1 = ((s8[5308416]{0:T(1024)(128)(4,1)}), s8[4194304]{0:T(1024)(128)(4,1)S(1)}, s32[]{:S(2)}) async-start(s8[5308416]{0:T(1024)(128)(4,1)} %bitcast.121), calls=%async_computation.1 | async-start | bytes 8388608
  289.5 31.1 %collective-permute-start.13 = (bf16[3,6,8,3,1536]{4,2,3,1,0:T(8,128)(2,1)}, bf16[3,6,8,3,1536]{4,2,3,1,0:T(8,128)(2,1)}, u32[]{:S(2)}, u32[]{:S(2)}) collective-permute-start(bf16[3,6,8,3,1536]{4,2,3,1,0:T(8,128)(2,1)} %copy.40), channel_id=1, source_target_pairs={{1,0},{2,1},{3,2},{4,3},{5,4},{6,5},{7,6},{8,7},{9,8},{10,9},{11,1... | collective-permute-start | bytes 3981320 | tf_op jit(solution)/shard_map/ppermute | solution.py:17
  291.9 34.2 %collective-permute-start.12 = (bf16[3,6,8,3,1536]{4,2,3,1,0:T(8,128)(2,1)}, bf16[3,6,8,3,1536]{4,2,3,1,0:T(8,128)(2,1)}, u32[]{:S(2)}, u32[]{:S(2)}) collective-permute-start(bf16[3,6,8,3,1536]{4,2,3,1,0:T(8,128)(2,1)} %copy.38), channel_id=1, source_target_pairs={{0,1},{1,2},{2,3},{3,4},{4,5},{5,6},{6,7},{7,8},{8,9},{9,10},{10,1... | collective-permute-start | bytes 3981320 | tf_op jit(solution)/shard_map/ppermute | solution.py:17
  295.4 8.9 %copy-start.1 = (bf16[1296,12,128]{2,0,1:T(8,128)(2,1)S(1)}, bf16[1296,12,128]{2,0,1:T(8,128)(2,1)}, u32[]{:S(2)}) copy-start(bf16[1296,12,128]{2,0,1:T(8,128)(2,1)} %copy.86) | copy-start | bytes 11943940
  295.4 8.9 %copy-start.9 = (bf16[4,144,1296]{2,1,0:T(8,128)(2,1)S(1)}, bf16[4,144,1296]{2,1,0:T(8,128)(2,1)}, u32[]{:S(2)}) copy-start(bf16[4,144,1296]{2,1,0:T(8,128)(2,1)} %copy-done.8) | copy-start | bytes 4478980
  295.7 9.2 %copy-start.11 = (bf16[4,144,1296]{2,1,0:T(8,128)(2,1)S(1)}, bf16[4,144,1296]{2,1,0:T(8,128)(2,1)}, u32[]{:S(2)}) copy-start(bf16[4,144,1296]{2,1,0:T(8,128)(2,1)} %copy-done.10) | copy-start | bytes 4478980
  297.1 8.5 %copy-start.13 = (bf16[4,144,1296]{2,1,0:T(8,128)(2,1)S(1)}, bf16[4,144,1296]{2,1,0:T(8,128)(2,1)}, u32[]{:S(2)}) copy-start(bf16[4,144,1296]{2,1,0:T(8,128)(2,1)} %copy-done.12) | copy-start | bytes 4478980
  297.1 51.9 %collective-permute-start.17 = (bf16[3,6,8,3,1536]{4,2,3,1,0:T(8,128)(2,1)}, bf16[3,6,8,3,1536]{4,2,3,1,0:T(8,128)(2,1)}, u32[]{:S(2)}, u32[]{:S(2)}) collective-permute-start(bf16[3,6,8,3,1536]{4,2,3,1,0:T(8,128)(2,1)} %copy.49), channel_id=1, source_target_pairs={{1,0},{2,1},{3,2},{4,3},{5,4},{6,5},{7,6},{8,7},{9,8},{10,9},{11,1... | collective-permute-start | bytes 3981320 | tf_op jit(solution)/shard_map/ppermute | solution.py:17
  303.0 51.2 %collective-permute-start.16 = (bf16[3,6,8,3,1536]{4,2,3,1,0:T(8,128)(2,1)S(1)}, bf16[3,6,8,3,1536]{4,2,3,1,0:T(8,128)(2,1)}, u32[]{:S(2)}, u32[]{:S(2)}) collective-permute-start(bf16[3,6,8,3,1536]{4,2,3,1,0:T(8,128)(2,1)S(1)} %copy.47), channel_id=1, source_target_pairs={{0,1},{1,2},{2,3},{3,4},{4,5},{5,6},{6,7},{7,8},{8,9},{9,10},{10,1... | collective-permute-start | bytes 3981320 | tf_op jit(solution)/shard_map/ppermute | solution.py:17
  331.1 32.5 %collective-permute-start.15 = (bf16[6,8,3,1536]{3,1,2,0:T(8,128)(2,1)S(1)}, bf16[6,8,3,1536]{3,1,2,0:T(8,128)(2,1)S(1)}, u32[]{:S(2)}, u32[]{:S(2)}) collective-permute-start(bf16[6,8,3,1536]{3,1,2,0:T(8,128)(2,1)S(1)} %copy.44), channel_id=1, source_target_pairs={{16,0},{32,16},{48,32},{64,48},{80,64},{96,80},{112,96},{128,112},... | collective-permute-start | bytes 1327112 | tf_op jit(solution)/shard_map/ppermute | solution.py:17
  333.1 30.6 %collective-permute-start.14 = (bf16[6,8,3,1536]{3,1,2,0:T(8,128)(2,1)S(1)}, bf16[6,8,3,1536]{3,1,2,0:T(8,128)(2,1)S(1)}, u32[]{:S(2)}, u32[]{:S(2)}) collective-permute-start(bf16[6,8,3,1536]{3,1,2,0:T(8,128)(2,1)S(1)} %copy.42), channel_id=1, source_target_pairs={{0,16},{16,32},{32,48},{48,64},{64,80},{80,96},{96,112},{112,128},... | collective-permute-start | bytes 1327112 | tf_op jit(solution)/shard_map/ppermute | solution.py:17
  359.3 7.7 %collective-permute-start.19 = (bf16[6,8,3,1536]{3,1,2,0:T(8,128)(2,1)S(1)}, bf16[6,8,3,1536]{3,1,2,0:T(8,128)(2,1)S(1)}, u32[]{:S(2)}, u32[]{:S(2)}) collective-permute-start(bf16[6,8,3,1536]{3,1,2,0:T(8,128)(2,1)S(1)} %copy.53), channel_id=1, source_target_pairs={{16,0},{32,16},{48,32},{64,48},{80,64},{96,80},{112,96},{128,112},... | collective-permute-start | bytes 1327112 | tf_op jit(solution)/shard_map/ppermute | solution.py:17
  361.2 11.7 %collective-permute-start.18 = (bf16[6,8,3,1536]{3,1,2,0:T(8,128)(2,1)S(1)}, bf16[6,8,3,1536]{3,1,2,0:T(8,128)(2,1)S(1)}, u32[]{:S(2)}, u32[]{:S(2)}) collective-permute-start(bf16[6,8,3,1536]{3,1,2,0:T(8,128)(2,1)S(1)} %copy.51), channel_id=1, source_target_pairs={{0,16},{16,32},{32,48},{48,64},{64,80},{80,96},{96,112},{112,128},... | collective-permute-start | bytes 1327112 | tf_op jit(solution)/shard_map/ppermute | solution.py:17
  (11 other events, 31.0 us)
where the time goes:
time: 380 us; the launch traced here: 375 us
  waiting for transfers between devices  131 us (34%)
  local copies, waits for them, and re-layouts  116 us (31%)
  starting transfers between devices  58.8 us (15%)
  matrix products  40 us (11%)
  other arithmetic  26 us (7%)
    ppermute x20, waiting for transfers between devices, passed_along(): return lax.ppermute(block, axis, route)  131 us
    ppermute x20, starting transfers between devices, passed_along(): return lax.ppermute(block, axis, route)  58.8 us
    another operation x8, local copies, waits for them, and re-layouts, head_major(): return block.reshape(block.shape[0], HEADS, HD).transpose(1, 0, 2)  38.9 us
    transpose x3, local copies, waits for them, and re-layouts, token_major(): return joined.transpose(1, 0, 2).reshape(joined.shape[1], HEADS * HD)  19.8 us
    dot_general x3, matrix products, attend_tile(): jnp.einsum('hqk,hqd->hkd', weights_low, grad_group, preferred_element_typ...  14.4 us
    another operation x1, local copies, waits for them, and re-layouts, on_device(): key_part = key_part.reshape(3, frames, 3, rows, columns, width)  12.2 us
    another operation x1, local copies, waits for them, and re-layouts, on_device(): value_part = value_part.reshape(3, frames, 3, rows, columns, width)  11.9 us
    dot_general x3, matrix products, attend_tile(): jnp.einsum('hqk,hkd->hqd', weights_low, value_group, preferred_element_ty...  10.6 us
  transfers between devices with their start and end apart: 20, of which 11 were waited for; matrix products, arithmetic and copies ran while one was open for 15% of the time, Pallas kernels for 0%

commit v1 on v0

v1 whole, which is shorter than its diff:
```python
import functools

import jax
import jax.numpy as jnp
from jax import lax
from jax.experimental import pallas as pl
from jax.experimental.pallas import tpu as pltpu
from jax.sharding import PartitionSpec as P

HEADS = 12
HD = 128
SLOTS = HEADS // 2
MESH = pl.DeviceIdType.MESH
F32 = jnp.float32
BF16 = jnp.bfloat16
LOG2E = 1.4426950408889634
MASKED = -1e30


def contract(lhs, rhs, lhs_dim, rhs_dim):
    return lax.dot_general(
        lhs, rhs, (((lhs_dim,), (rhs_dim,)), ((), ())), preferred_element_type=F32
    )


def key_bias(frame_counts, row_counts, time_reach, row_reach, n_time, n_row, frames, rows, tokens):
    count = n_time * n_row * tokens
    lane = lax.broadcasted_iota(jnp.int32, (1, count), 1)

    def steps(position, step, limit):
        total = jnp.zeros_like(position)
        for k in range(1, limit):
            total = total + jnp.where(position >= k * step, 1, 0)
        return total

    time_tile = steps(lane, n_row * tokens, n_time)
    in_time = lane - time_tile * (n_row * tokens)
    row_tile = steps(in_time, tokens, n_row)
    token = in_time - row_tile * tokens
    frame = steps(token, tokens // frames, frames)
    row = lane & (rows - 1)

    def picked(tile, counts, reach):
        if len(counts) == 1:
            return counts[0]
        outer = jnp.where(reach > 0, 1, 0)
        return jnp.where(
            tile == 1, counts[1], jnp.where(tile == 0, counts[0], counts[2]) * outer
        )

    inside = (frame < picked(time_tile, frame_counts, time_reach)) & (
        row < picked(row_tile, row_counts, row_reach)
    )
    return jnp.where(inside, 0.0, MASKED).astype(F32)


def attend(query, key, value, grad, bias):
    scale = HD**-0.5
    scores = contract(query, key, 1, 1) + bias
    row_max = jnp.max(scores, axis=1, keepdims=True)
    raised = jnp.exp2((scores - row_max) * (scale * LOG2E))
    weights = raised * (1.0 / jnp.sum(raised, axis=1, keepdims=True))
    weights_low = weights.astype(BF16)
    output = contract(weights_low, value, 1, 0).astype(BF16).astype(F32)
    row_delta = jnp.sum(output * grad.astype(F32), axis=1, keepdims=True)
    grad_weights = contract(grad, value, 1, 1)
    grad_low = (weights * (grad_weights - row_delta)).astype(BF16)
    grad_query = contract(grad_low, key, 1, 0) * scale
    grad_key = contract(grad_low, query, 0, 0) * scale
    grad_value = contract(weights_low, grad, 0, 0)
    return grad_query, grad_key, grad_value


def kernel(
    full, high, dims,
    perm, place, radius, fv, rv, q_in, k_in, v_in, g_in, dq_out, dk_out, dv_out,
    qg, kv, part, ret_y, ret_z, z_out, sums, result, stage, heads, frame_counts, row_counts,
    swap_s, swap_r, z_s, z_r, y_s, y_r, c_s, c_r, ry_s, ry_r, rz_s, rz_r, back_s, back_r,
    n_s, n_r,
):
    frames, rows, tokens, n_tm, n_height = dims
    tm = lax.axis_index("tm")
    height = lax.axis_index("height")
    chip = tm // 2
    core = tm % 2
    other = 1 - core
    sibling = (chip * 2 + other, height)
    z_next = ((tm + 2) % n_tm, height)
    z_prev = ((tm + n_tm - 2) % n_tm, height)
    y_next = (tm, (height + 1) % n_height)
    y_prev = (tm, (height + n_height - 1) % n_height)
    z_dev = (z_next, z_prev)
    y_dev = (y_next, y_prev)
    mid = pl.ds(tokens, tokens)

    def remote(src, dst, send, recv, device):
        return pltpu.make_async_remote_copy(
            src_ref=src, dst_ref=dst, send_sem=send, recv_sem=recv,
            device_id=device, device_id_type=MESH,
        )

    barrier = pltpu.get_barrier_semaphore()
    for device in (sibling, z_next, z_prev, y_next, y_prev):
        pl.semaphore_signal(barrier, inc=1, device_id=device, device_id_type=MESH)

    frame_counts[1 + core] = jnp.full((8, 128), fv[0], jnp.int32)
    row_counts[1] = jnp.full((8, 128), rv[0], jnp.int32)

    for head in range(HEADS):
        lanes = pl.ds(head * HD, HD)
        for index, source in enumerate((k_in, v_in, q_in, g_in)):
            heads[head, index] = source[:, lanes]

    def pack(slot, _):
        theirs = perm[2 * slot + other]
        mine = perm[2 * slot + core]
        stage[slot] = heads[theirs]
        block = heads[mine]
        kv[slot, 0, 1 + core, mid] = block[0]
        kv[slot, 1, 1 + core, mid] = block[1]
        qg[slot, 0, core] = block[2]
        qg[slot, 1, core] = block[3]
        return 0

    lax.fori_loop(0, SLOTS, pack, 0)
    pl.semaphore_wait(barrier, 5)

    def counts_swap():
        return remote(
            frame_counts.at[1 + core], frame_counts.at[1 + core], n_s.at[0], n_r.at[0], sibling
        )

    def counts_z(way):
        return remote(
            frame_counts.at[2 - way], frame_counts.at[3 * way], n_s.at[1 + way], n_r.at[1 + way],
            z_dev[way],
        )

    def counts_y(way):
        return remote(
            row_counts.at[1], row_counts.at[2 * way], n_s.at[3 + way], n_r.at[3 + way], y_dev[way]
        )

    def swap_kv(slot):
        return remote(
            stage.at[slot, pl.ds(0, 2)], kv.at[slot, :, 1 + core, mid], swap_s.at[0, slot],
            swap_r.at[0, slot], sibling,
        )

    def swap_qg(slot):
        return remote(
            stage.at[slot, pl.ds(2, 2)], qg.at[slot, :, core], swap_s.at[1, slot],
            swap_r.at[1, slot], sibling,
        )

    def send_z(slot, way):
        return remote(
            kv.at[slot, :, 2 - way, mid], kv.at[slot, :, 3 * way, mid], z_s.at[way, slot],
            z_r.at[way, slot], z_dev[way],
        )

    def send_y(slot, way):
        return remote(
            kv.at[slot, :, pl.ds(1, 2), mid],
            kv.at[slot, :, pl.ds(1, 2), pl.ds(2 * way * tokens, tokens)],
            y_s.at[way, slot], y_r.at[way, slot], y_dev[way],
        )

    def send_corner(slot, way, side):
        return remote(
            kv.at[slot, :, 3 * side, mid],
            kv.at[slot, :, 3 * side, pl.ds(2 * way * tokens, tokens)],
            c_s.at[way, side, slot], c_r.at[way, side, slot], y_dev[way],
        )

    def return_y(slot, way, time):
        return remote(
            part.at[slot, :, time, pl.ds(2 * (1 - way) * tokens, tokens)],
            ret_y.at[way, slot, :, time],
            ry_s.at[way, slot], ry_r.at[way, slot], y_dev[way],
        )

    def return_z(slot, way):
        return remote(
            z_out.at[way, slot], ret_z.at[way, slot], rz_s.at[way, slot], rz_r.at[way, slot],
            z_dev[way],
        )

    def send_back(slot):
        return remote(
            result.at[2 * SLOTS + slot], result.at[core * SLOTS + slot], back_s.at[slot], back_r.at[slot], sibling
        )

    counts_swap().start()
    for way in range(2):
        counts_y(way).start()

    def loop(start, stop, body):
        if stop > start:
            def step(slot, _):
                body(slot)
                return 0
            lax.fori_loop(start, stop, step, 0)

    loop(0, SLOTS, lambda slot: swap_kv(slot).start())
    loop(0, SLOTS, lambda slot: swap_qg(slot).start())
    counts_swap().wait_recv()
    for way in range(2):
        counts_z(way).start()

    def first_full(slot):
        swap_kv(slot).wait_recv()
        for way in range(2):
            send_z(slot, way).start()
        for way in range(2):
            send_y(slot, way).start()

    def first_high(slot):
        swap_kv(slot).wait_recv()
        for way in range(2):
            send_y(slot, way).start()

    def first_wide(slot):
        swap_kv(slot).wait_recv()
        for way in range(2):
            send_z(slot, way).start()

    loop(0, full, first_full)
    loop(high, SLOTS, first_wide)
    loop(full, high, first_high)

    def corners(slot):
        for side in range(2):
            send_z(slot, side).wait_recv()
            for way in range(2):
                send_corner(slot, way, side).start()

    loop(0, full, corners)

    for way in range(2):
        counts_z(way).wait_recv()
        counts_y(way).wait_recv()

    edges_time = (
        jnp.where(chip > 0, 1, 0), 1, 1, jnp.where(chip < n_tm // 2 - 1, 1, 0)
    )
    edges_row = (
        jnp.where(height > 0, 1, 0), 1, jnp.where(height < n_height - 1, 1, 0)
    )

    def frame_count(time):
        return frame_counts[time, 0:1, 0:1] * edges_time[time]

    def row_count(row):
        return row_counts[row, 0:1, 0:1] * edges_row[row]

    def compute(slot, n_time, n_row):
        time_reach, row_reach = radius[0, 2 * slot + core], radius[1, 2 * slot + core]
        swap_qg(slot).wait_recv()
        first_row = 0 if n_row == 3 else 1
        key_parts = []
        value_parts = []
        for tile in range(2):
            first_time = tile if n_time == 3 else tile + 1
            bias = key_bias(
                [frame_count(first_time + k) for k in range(n_time)],
                [row_count(first_row + k) for k in range(n_row)],
                time_reach, row_reach, n_time, n_row, frames, rows, tokens,
            )
            span = (pl.ds(first_time, n_time), pl.ds(first_row * tokens, n_row * tokens))
            count = n_time * n_row * tokens
            key = kv[slot, 0, span[0], span[1]].reshape(count, HD)
            value = kv[slot, 1, span[0], span[1]].reshape(count, HD)
            grad_query, grad_key, grad_value = attend(
                qg[slot, 0, tile], key, value, qg[slot, 1, tile], bias
            )
            low = grad_query.astype(BF16)

            @pl.when(core == tile)
            def _(low=low):
                result[core * SLOTS + slot, 0] = low

            @pl.when(core != tile)
            def _(low=low):
                result[2 * SLOTS + slot, 0] = low

            key_parts.append(grad_key)
            value_parts.append(grad_value)
        where = pl.ds(first_row * tokens, n_row * tokens)
        width = n_row * tokens
        for kind, parts in ((0, key_parts), (1, value_parts)):
            if n_time == 3:
                part[slot, kind, 0, where] = parts[0][:width].astype(BF16)
                for time in (1, 2):
                    part[slot, kind, time, where] = (
                        parts[0][time * width : (time + 1) * width]
                        + parts[1][(time - 1) * width : time * width]
                    ).astype(BF16)
                part[slot, kind, 3, where] = parts[1][2 * width :].astype(BF16)
            else:
                part[slot, kind, 1, where] = parts[0].astype(BF16)
                part[slot, kind, 2, where] = parts[1].astype(BF16)

    every = pl.ds(0, 4)
    own = pl.ds(1, 2)

    def compute_full(slot):
        for way in range(2):
            send_y(slot, way).wait_recv()
            for side in range(2):
                send_corner(slot, way, side).wait_recv()
        compute(slot, 3, 3)
        for way in range(2):
            return_y(slot, way, every).start()

    def compute_high(slot):
        for way in range(2):
            send_y(slot, way).wait_recv()
        compute(slot, 1, 3)
        for way in range(2):
            return_y(slot, way, own).start()

    def compute_wide(slot):
        for way in range(2):
            send_z(slot, way).wait_recv()
        compute(slot, 3, 1)
        for kind in range(2):
            for time in (1, 2):
                sums[slot, kind, time - 1] = part[slot, kind, time, mid].astype(F32)
            z_out[0, slot, kind] = part[slot, kind, 3, mid]
            z_out[1, slot, kind] = part[slot, kind, 0, mid]
        for way in range(2):
            return_z(slot, way).start()

    loop(high, SLOTS, compute_wide)
    loop(0, full, compute_full)
    loop(full, high, compute_high)

    def reduced(slot, kind, time):
        return (
            part[slot, kind, time, mid].astype(F32)
            + ret_y[0, slot, kind, time].astype(F32)
            + ret_y[1, slot, kind, time].astype(F32)
        )

    def reduce_full(slot):
        for way in range(2):
            return_y(slot, way, every).wait_recv()
        for kind in range(2):
            for time in (1, 2):
                sums[slot, kind, time - 1] = reduced(slot, kind, time)
            z_out[0, slot, kind] = reduced(slot, kind, 3).astype(BF16)
            z_out[1, slot, kind] = reduced(slot, kind, 0).astype(BF16)
        for way in range(2):
            return_z(slot, way).start()

    def reduce_high(slot):
        for way in range(2):
            return_y(slot, way, own).wait_recv()
        for kind in range(2):
            for time in (1, 2):
                sums[slot, kind, time - 1] = reduced(slot, kind, time)

    loop(0, full, reduce_full)
    loop(full, high, reduce_high)

    def finish(slot, with_z):
        if with_z:
            for way in range(2):
                return_z(slot, way).wait_recv()
        for kind in range(2):
            for tile in range(2):
                total = sums[slot, kind, tile]
                if with_z:
                    total = total + ret_z[tile, slot, kind].astype(F32)
                low = total.astype(BF16)

                @pl.when(core == tile)
                def _(low=low, kind=kind):
                    result[core * SLOTS + slot, 1 + kind] = low

                @pl.when(core != tile)
                def _(low=low, kind=kind):
                    result[2 * SLOTS + slot, 1 + kind] = low

        send_back(slot).start()

    loop(full, high, lambda slot: finish(slot, False))
    loop(high, SLOTS, lambda slot: finish(slot, True))
    loop(0, full, lambda slot: finish(slot, True))

    def drain(slot):
        swap_kv(slot).wait_send()
        swap_qg(slot).wait_send()
        send_back(slot).wait_send()

    def drain_z(slot):
        for way in range(2):
            send_z(slot, way).wait_send()
            return_z(slot, way).wait_send()

    def drain_y(slot, time):
        for way in range(2):
            send_y(slot, way).wait_send()
            return_y(slot, way, time).wait_send()

    def drain_corner(slot):
        for way in range(2):
            for side in range(2):
                send_corner(slot, way, side).wait_send()

    loop(0, SLOTS, drain)
    loop(0, full, drain_z)
    loop(high, SLOTS, drain_z)
    loop(0, full, lambda slot: drain_y(slot, every))
    loop(full, high, lambda slot: drain_y(slot, own))
    loop(0, full, drain_corner)
    counts_swap().wait_send()
    for way in range(2):
        counts_z(way).wait_send()
        counts_y(way).wait_send()

    loop(0, SLOTS, lambda slot: send_back(slot).wait_recv())

    for head in range(HEADS):
        lanes = pl.ds(head * HD, HD)
        where = place[head]
        block = result[where]
        dq_out[:, lanes] = block[0]
        dk_out[:, lanes] = block[1]
        dv_out[:, lanes] = block[2]


def tile_call(full, high, dims, collective_id, operands):
    frames, rows, tokens, n_tm, n_height = dims
    width = HEADS * HD
    smem = pl.BlockSpec(memory_space=pltpu.SMEM)
    vmem = pl.BlockSpec(memory_space=pltpu.VMEM)
    dma = pltpu.SemaphoreType.DMA
    tile = (tokens, HD)
    out = jax.ShapeDtypeStruct((tokens, width), BF16)
    return pl.pallas_call(
        functools.partial(kernel, full, high, dims),
        out_shape=(out, out, out),
        in_specs=[smem] * 5 + [vmem] * 4,
        out_specs=(vmem, vmem, vmem),
        scratch_shapes=[
            pltpu.VMEM((SLOTS, 2, 2) + tile, BF16),
            pltpu.VMEM((SLOTS, 2, 4, 3 * tokens, HD), BF16),
            pltpu.VMEM((SLOTS, 2, 4, 3 * tokens, HD), BF16),
            pltpu.VMEM((2, SLOTS, 2, 4) + tile, BF16),
            pltpu.VMEM((2, SLOTS, 2) + tile, BF16),
            pltpu.VMEM((2, SLOTS, 2) + tile, BF16),
            pltpu.VMEM((SLOTS, 2, 2) + tile, F32),
            pltpu.VMEM((3 * SLOTS, 3) + tile, BF16),
            pltpu.VMEM((SLOTS, 4) + tile, BF16),
            pltpu.VMEM((HEADS, 4) + tile, BF16),
            pltpu.VMEM((4, 8, 128), jnp.int32),
            pltpu.VMEM((3, 8, 128), jnp.int32),
            dma((2, SLOTS)), dma((2, SLOTS)),
            dma((2, SLOTS)), dma((2, SLOTS)),
            dma((2, SLOTS)), dma((2, SLOTS)),
            dma((2, 2, SLOTS)), dma((2, 2, SLOTS)),
            dma((2, SLOTS)), dma((2, SLOTS)),
            dma((2, SLOTS)), dma((2, SLOTS)),
            dma((SLOTS,)), dma((SLOTS,)),
            dma((5,)), dma((5,)),
        ],
        compiler_params=pltpu.CompilerParams(
            collective_id=collective_id, has_side_effects=True, vmem_limit_bytes=56 << 20
        ),
        cost_estimate=pl.CostEstimate(
            flops=2 * 6 * tokens * 9 * tokens * width, bytes_accessed=7 * 2 * tokens * width,
            transcendentals=9 * tokens * tokens * HEADS,
        ),
    )(*operands)


def on_device(queries, keys, values, grad_out, window_radius, frames_valid, rows_valid):
    frames, rows, columns, width = queries.shape
    tokens = frames * rows * columns

    def flat(block):
        return block.transpose(0, 2, 1, 3).reshape(tokens, width)

    def unflat(block):
        return block.reshape(frames, columns, rows, width).transpose(0, 2, 1, 3)

    dims = (frames, rows, tokens, lax.axis_size("tm"), lax.axis_size("height"))
    time_reach, row_reach = window_radius[:, 0], window_radius[:, 1]
    kind = jnp.where(row_reach > 0, 1 - time_reach, 2 + time_reach)
    heads = jnp.arange(HEADS, dtype=jnp.int32)
    order = kind * HEADS + heads
    rank = jnp.sum((order[None, :] < order[:, None]).astype(jnp.int32), axis=1)
    perm = jnp.sum(jnp.where(rank[None, :] == heads[:, None], heads[None, :], 0), axis=1)
    reach = jnp.sum(
        jnp.where(rank[None, None, :] == heads[None, :, None], window_radius.T[:, None, :], 0), axis=2
    )
    place = (rank % 2) * SLOTS + rank // 2
    operands = (
        perm, place, reach, frames_valid, rows_valid,
        flat(queries), flat(keys), flat(values), flat(grad_out),
    )
    outs = tile_call(SLOTS, SLOTS, dims, 0, operands)
    return tuple(unflat(out) for out in outs)


def solution(mesh):
    placed = P("tm", "height", None, None)
    return jax.shard_map(
        on_device,
        mesh=mesh,
        in_specs=(placed, placed, placed, placed, P(), P("tm"), P("height")),
        out_specs=(placed, placed, placed),
        check_vma=False,
    )
```

time: 380 us -> 194 us (0.51)
  the two profiles are of different devices: /device:TPU:382 before, /device:TPU:1 now
where the time goes in v1:
time: 194 us; the launch traced here: 191 us
  Pallas kernels  183 us (94%)
  local copies, waits for them, and re-layouts  5.12 us (3%)
  between operations  1.96 us (1%)
    pallas_call x1, Pallas kernels, tile_call(): pl.pallas_call(functools.partial(kernel, full, high, dims), out_shape=(ou...  183 us
    unnamed x9, local copies, waits for them, and re-layouts  4.47 us

profile of v1, /device:TPU:1, one launch (start us, length us, event | category | flops | bytes accessed | tf_op | source)
XLA Modules:
  0.0 191.3 jit_solution(5169462999967523166)
XLA Ops:
  1.9 0.0 copy-start.2
  1.9 0.7 copy-done.2
  2.6 0.2 convert_reduce_fusion
  2.8 0.6 select_reduce_fusion.1.perm
  3.4 0.5 fusion.2.place
  4.0 0.3 select_reduce_fusion
  4.2 0.6 copy.10.radius
  4.9 182.6 %shard_map.94 = (bf16[144,1536]{1,0:T(8,128)(2,1)}, bf16[144,1536]{1,0:T(8,128)(2,1)}, bf16[144,1536]{1,0:T(8,128)(2,1)}) custom-call(s32[12]{0:T(128)} %select_reduce_fusion.1.perm, s32[12]{0:T(128)} %fusion.2.place, s32[2,12]{1,0:T(2,128)} %copy.10.radius, s32[1]{0:T(128)S(6)} %copy.14.fv, s32[1]{0:T(128)S(6)} %copy.15.rv, bf16[144,1536]{1,0:T(8,128)(2,1)} %bitcast.30, ...), custom_call_target="tpu_custom_call" | custom-call | flops 3439853568 | bytes 3096576 | tf_op jit(solution)/shard_map/pallas_call | solution.py:442
  187.5 0.0 copy-start.1
  187.5 1.9 copy.16
  189.4 0.0 copy-done.1
  189.4 0.0 copy-start
  189.4 0.8 copy.17
  190.1 0.4 copy-done
  190.6 0.8 copy.18
  (3 shorter events, 0.0 us)
Async XLA Ops:
  1.9 0.7 copy-start.2
  187.5 1.9 copy-start.1
  189.4 1.2 copy-start

commit v2 on v1

--- a/solution.py
+++ b/solution.py
@@ -10,6 +10,7 @@
 HEADS = 12
 HD = 128
 SLOTS = HEADS // 2
+PLANS = ((2, 4), (3, 5), (SLOTS, SLOTS))
 MESH = pl.DeviceIdType.MESH
 F32 = jnp.float32
 BF16 = jnp.bfloat16
@@ -75,7 +76,7 @@
     full, high, dims,
     perm, place, radius, fv, rv, q_in, k_in, v_in, g_in, dq_out, dk_out, dv_out,
     qg, kv, part, ret_y, ret_z, z_out, sums, result, stage, heads, frame_counts, row_counts,
-    swap_s, swap_r, z_s, z_r, y_s, y_r, c_s, c_r, ry_s, ry_r, rz_s, rz_r, back_s, back_r,
+    swap_s, swap_r, z_s, z_r, y_s, y_r, ry_s, ry_r, rz_s, rz_r, back_s, back_r,
     n_s, n_r,
 ):
     frames, rows, tokens, n_tm, n_height = dims
@@ -91,7 +92,20 @@
     y_prev = (tm, (height + n_height - 1) % n_height)
     z_dev = (z_next, z_prev)
     y_dev = (y_next, y_prev)
-    mid = pl.ds(tokens, tokens)
+    half = n_height // 2
+    relay = (height == n_height - 1, height == 0)
+    entry = (height == half - 1, height == half)
+    far = (
+        (tm, jnp.where(entry[0], n_height - 1, jnp.where(relay[0], half, height + 1))),
+        (tm, jnp.where(entry[1], 0, jnp.where(relay[1], half - 1, height - 1))),
+    )
+    land = (jnp.where(entry[0], 1, 0), jnp.where(entry[1], 0, 1))
+    origin = (jnp.where(relay[0], 2, 1), jnp.where(relay[1], 0, 1))
+    special = relay[0] | relay[1] | entry[0] | entry[1]
+    upper = height >= half
+    at_end = relay[0] | relay[1]
+    greet_first = jnp.where(at_end, jnp.where(upper, half - 1, half), jnp.where(upper, 0, n_height - 1))
+    greet_second = jnp.where(at_end, jnp.where(upper, half, half - 1), jnp.where(upper, n_height - 1, 0))
 
     def remote(src, dst, send, recv, device):
         return pltpu.make_async_remote_copy(
@@ -102,6 +116,11 @@
     barrier = pltpu.get_barrier_semaphore()
     for device in (sibling, z_next, z_prev, y_next, y_prev):
         pl.semaphore_signal(barrier, inc=1, device_id=device, device_id_type=MESH)
+
+    @pl.when(special)
+    def _():
+        for device in ((tm, greet_first), (tm, greet_second)):
+            pl.semaphore_signal(barrier, inc=1, device_id=device, device_id_type=MESH)
 
     frame_counts[1 + core] = jnp.full((8, 128), fv[0], jnp.int32)
     row_counts[1] = jnp.full((8, 128), rv[0], jnp.int32)
@@ -116,14 +135,30 @@
         mine = perm[2 * slot + core]
         stage[slot] = heads[theirs]
         block = heads[mine]
-        kv[slot, 0, 1 + core, mid] = block[0]
-        kv[slot, 1, 1 + core, mid] = block[1]
+        kv[slot, 0, 1 + core, 1] = block[0]
+        kv[slot, 1, 1 + core, 1] = block[1]
         qg[slot, 0, core] = block[2]
         qg[slot, 1, core] = block[3]
         return 0
 
     lax.fori_loop(0, SLOTS, pack, 0)
-    pl.semaphore_wait(barrier, 5)
+
+    for way in range(2):
+        @pl.when(relay[way])
+        def _(way=way):
+            def clear(slot, _):
+                kv[slot, 0, :, 2 * (1 - way)] = jnp.zeros((4, tokens, HD), BF16)
+                return 0
+
+            lax.fori_loop(0, SLOTS, clear, 0)
+
+    @pl.when(special)
+    def _():
+        pl.semaphore_wait(barrier, 7)
+
+    @pl.when(jnp.logical_not(special))
+    def _():
+        pl.semaphore_wait(barrier, 5)
 
     def counts_swap():
         return remote(
@@ -143,7 +178,7 @@
 
     def swap_kv(slot):
         return remote(
-            stage.at[slot, pl.ds(0, 2)], kv.at[slot, :, 1 + core, mid], swap_s.at[0, slot],
+            stage.at[slot, pl.ds(0, 2)], kv.at[slot, :, 1 + core, 1], swap_s.at[0, slot],
             swap_r.at[0, slot], sibling,
         )
 
@@ -155,30 +190,87 @@
 
     def send_z(slot, way):
         return remote(
-            kv.at[slot, :, 2 - way, mid], kv.at[slot, :, 3 * way, mid], z_s.at[way, slot],
+            kv.at[slot, :, 2 - way, 1], kv.at[slot, :, 3 * way, 1], z_s.at[way, slot],
             z_r.at[way, slot], z_dev[way],
         )
 
-    def send_y(slot, way):
-        return remote(
-            kv.at[slot, :, pl.ds(1, 2), mid],
-            kv.at[slot, :, pl.ds(1, 2), pl.ds(2 * way * tokens, tokens)],
-            y_s.at[way, slot], y_r.at[way, slot], y_dev[way],
-        )
-
-    def send_corner(slot, way, side):
-        return remote(
-            kv.at[slot, :, 3 * side, mid],
-            kv.at[slot, :, 3 * side, pl.ds(2 * way * tokens, tokens)],
-            c_s.at[way, side, slot], c_r.at[way, side, slot], y_dev[way],
-        )
-
-    def return_y(slot, way, time):
-        return remote(
-            part.at[slot, :, time, pl.ds(2 * (1 - way) * tokens, tokens)],
-            ret_y.at[way, slot, :, time],
-            ry_s.at[way, slot], ry_r.at[way, slot], y_dev[way],
-        )
+    times = (pl.ds(1, 2), pl.ds(0, 1), pl.ds(3, 1))
+
+    def send_y(slot, way, kind, group):
+        time = times[group]
+        start, stop, device = (1, way, y_dev[way]) if kind == 0 else (origin[way], land[way], far[way])
+        return remote(
+            kv.at[slot, kind, time, start], kv.at[slot, kind, time, 2 * stop],
+            y_s.at[group, kind, way, slot], y_r.at[group, kind, stop, slot], device,
+        )
+
+    def arrive_y(slot, way, kind, group):
+        time = times[group]
+        return remote(
+            kv.at[slot, kind, time, 1], kv.at[slot, kind, time, 2 * way],
+            y_s.at[group, kind, way, slot], y_r.at[group, kind, way, slot], y_dev[way],
+        )
+
+    def start_y(slot, group):
+        for way in range(2):
+            @pl.when(jnp.logical_not(relay[way]))
+            def _(way=way):
+                send_y(slot, way, 0, group).start()
+                send_y(slot, way, 1, group).start()
+
+        for way in range(2):
+            @pl.when(relay[way])
+            def _(way=way):
+                arrive_y(slot, 1 - way, 1, group).wait_recv()
+                send_y(slot, way, 1, group).start()
+
+    def wait_y(slot, groups):
+        for way in range(2):
+            @pl.when(jnp.logical_not(relay[1 - way]))
+            def _(way=way):
+                for group in groups:
+                    for kind in range(2):
+                        arrive_y(slot, way, kind, group).wait_recv()
+
+    def return_y(slot, way, kind, time):
+        stop, device = (way, y_dev[way]) if kind == 0 else (land[way], far[way])
+        return remote(
+            part.at[slot, kind, time, 2 * (1 - way)], ret_y.at[stop, slot, kind, time],
+            ry_s.at[kind, way, slot], ry_r.at[kind, stop, slot], device,
+        )
+
+    def returned_y(slot, way, kind, time):
+        return remote(
+            part.at[slot, kind, time, 2 * (1 - way)], ret_y.at[way, slot, kind, time],
+            ry_s.at[kind, way, slot], ry_r.at[kind, way, slot], y_dev[way],
+        )
+
+    def relay_y(slot, way, time):
+        return remote(
+            ret_y.at[1 - way, slot, 1, time], ret_y.at[way, slot, 1, time],
+            ry_s.at[1, way, slot], ry_r.at[1, way, slot], far[way],
+        )
+
+    def start_return(slot, time):
+        for way in range(2):
+            @pl.when(jnp.logical_not(relay[way]))
+            def _(way=way):
+                for kind in range(2):
+                    return_y(slot, way, kind, time).start()
+
+    def pass_return(slot, time):
+        for way in range(2):
+            @pl.when(relay[way])
+            def _(way=way):
+                returned_y(slot, 1 - way, 1, time).wait_recv()
+                relay_y(slot, way, time).start()
+
+    def wait_return(slot, time):
+        for way in range(2):
+            @pl.when(jnp.logical_not(relay[1 - way]))
+            def _(way=way):
+                for kind in range(2):
+                    returned_y(slot, way, kind, time).wait_recv()
 
     def return_z(slot, way):
         return remote(
@@ -188,7 +280,8 @@
 
     def send_back(slot):
         return remote(
-            result.at[2 * SLOTS + slot], result.at[core * SLOTS + slot], back_s.at[slot], back_r.at[slot], sibling
+            result.at[2 * SLOTS + slot], result.at[core * SLOTS + slot], back_s.at[slot],
+            back_r.at[slot], sibling,
         )
 
     counts_swap().start()
@@ -208,34 +301,28 @@
     for way in range(2):
         counts_z(way).start()
 
-    def first_full(slot):
+    def first_z(slot):
         swap_kv(slot).wait_recv()
         for way in range(2):
             send_z(slot, way).start()
-        for way in range(2):
-            send_y(slot, way).start()
-
-    def first_high(slot):
-        swap_kv(slot).wait_recv()
-        for way in range(2):
-            send_y(slot, way).start()
-
-    def first_wide(slot):
-        swap_kv(slot).wait_recv()
-        for way in range(2):
-            send_z(slot, way).start()
-
-    loop(0, full, first_full)
-    loop(high, SLOTS, first_wide)
-    loop(full, high, first_high)
+
+    loop(0, full, first_z)
+    loop(full, high, lambda slot: swap_kv(slot).wait_recv())
+    loop(high, SLOTS, first_z)
+    if full:
+        start_y(0, 0)
 
     def corners(slot):
+        @pl.when(slot + 1 < full)
+        def _():
+            start_y(slot + 1, 0)
+
         for side in range(2):
             send_z(slot, side).wait_recv()
-            for way in range(2):
-                send_corner(slot, way, side).start()
+            start_y(slot, 1 + side)
 
     loop(0, full, corners)
+    loop(full, high, lambda slot: start_y(slot, 0))
 
     for way in range(2):
         counts_z(way).wait_recv()
@@ -267,7 +354,7 @@
                 [row_count(first_row + k) for k in range(n_row)],
                 time_reach, row_reach, n_time, n_row, frames, rows, tokens,
             )
-            span = (pl.ds(first_time, n_time), pl.ds(first_row * tokens, n_row * tokens))
+            span = (pl.ds(first_time, n_time), pl.ds(first_row, n_row))
             count = n_time * n_row * tokens
             key = kv[slot, 0, span[0], span[1]].reshape(count, HD)
             value = kv[slot, 1, span[0], span[1]].reshape(count, HD)
@@ -286,39 +373,46 @@
 
             key_parts.append(grad_key)
             value_parts.append(grad_value)
-        where = pl.ds(first_row * tokens, n_row * tokens)
+        where = pl.ds(first_row, n_row)
         width = n_row * tokens
+
+        def put(kind, time, total):
+            part[slot, kind, time, where] = total.astype(BF16).reshape(n_row, tokens, HD)
+
         for kind, parts in ((0, key_parts), (1, value_parts)):
             if n_time == 3:
-                part[slot, kind, 0, where] = parts[0][:width].astype(BF16)
+                put(kind, 0, parts[0][:width])
                 for time in (1, 2):
-                    part[slot, kind, time, where] = (
+                    put(
+                        kind, time,
                         parts[0][time * width : (time + 1) * width]
-                        + parts[1][(time - 1) * width : time * width]
-                    ).astype(BF16)
-                part[slot, kind, 3, where] = parts[1][2 * width :].astype(BF16)
+                        + parts[1][(time - 1) * width : time * width],
+                    )
+                put(kind, 3, parts[1][2 * width :])
             else:
-                part[slot, kind, 1, where] = parts[0].astype(BF16)
-                part[slot, kind, 2, where] = parts[1].astype(BF16)
+                put(kind, 1, parts[0])
+                put(kind, 2, parts[1])
 
     every = pl.ds(0, 4)
     own = pl.ds(1, 2)
 
     def compute_full(slot):
-        for way in range(2):
-            send_y(slot, way).wait_recv()
-            for side in range(2):
-                send_corner(slot, way, side).wait_recv()
+        wait_y(slot, (0, 1, 2))
         compute(slot, 3, 3)
-        for way in range(2):
-            return_y(slot, way, every).start()
+        start_return(slot, every)
+
+        @pl.when(slot > 0)
+        def _():
+            pass_return(slot - 1, every)
 
     def compute_high(slot):
-        for way in range(2):
-            send_y(slot, way).wait_recv()
+        wait_y(slot, (0,))
         compute(slot, 1, 3)
-        for way in range(2):
-            return_y(slot, way, own).start()
+        start_return(slot, own)
+
+        @pl.when(slot > full)
+        def _():
+            pass_return(slot - 1, own)
 
     def compute_wide(slot):
         for way in range(2):
@@ -326,26 +420,29 @@
         compute(slot, 3, 1)
         for kind in range(2):
             for time in (1, 2):
-                sums[slot, kind, time - 1] = part[slot, kind, time, mid].astype(F32)
-            z_out[0, slot, kind] = part[slot, kind, 3, mid]
-            z_out[1, slot, kind] = part[slot, kind, 0, mid]
+                sums[slot, kind, time - 1] = part[slot, kind, time, 1].astype(F32)
+            z_out[0, slot, kind] = part[slot, kind, 3, 1]
+            z_out[1, slot, kind] = part[slot, kind, 0, 1]
         for way in range(2):
             return_z(slot, way).start()
 
     loop(high, SLOTS, compute_wide)
     loop(0, full, compute_full)
+    if full:
+        pass_return(full - 1, every)
     loop(full, high, compute_high)
+    if high > full:
+        pass_return(high - 1, own)
 
     def reduced(slot, kind, time):
-        return (
-            part[slot, kind, time, mid].astype(F32)
-            + ret_y[0, slot, kind, time].astype(F32)
-            + ret_y[1, slot, kind, time].astype(F32)
-        )
+        total = part[slot, kind, time, 1].astype(F32)
+        for way in range(2):
+            block = ret_y[way, slot, kind, time].astype(F32)
+            total = total + jnp.where(relay[1 - way], 0.0, block)
+        return total
 
     def reduce_full(slot):
-        for way in range(2):
-            return_y(slot, way, every).wait_recv()
+        wait_return(slot, every)
         for kind in range(2):
             for time in (1, 2):
                 sums[slot, kind, time - 1] = reduced(slot, kind, time)
@@ -355,8 +452,7 @@
             return_z(slot, way).start()
 
     def reduce_high(slot):
-        for way in range(2):
-            return_y(slot, way, own).wait_recv()
+        wait_return(slot, own)
         for kind in range(2):
             for time in (1, 2):
                 sums[slot, kind, time - 1] = reduced(slot, kind, time)
@@ -399,22 +495,23 @@
             send_z(slot, way).wait_send()
             return_z(slot, way).wait_send()
 
-    def drain_y(slot, time):
-        for way in range(2):
-            send_y(slot, way).wait_send()
-            return_y(slot, way, time).wait_send()
-
-    def drain_corner(slot):
-        for way in range(2):
-            for side in range(2):
-                send_corner(slot, way, side).wait_send()
+    def drain_y(slot, groups, time):
+        for way in range(2):
+            @pl.when(jnp.logical_not(relay[way]))
+            def _(way=way):
+                for group in groups:
+                    send_y(slot, way, 0, group).wait_send()
+                return_y(slot, way, 0, time).wait_send()
+
+            for group in groups:
+                send_y(slot, way, 1, group).wait_send()
+            return_y(slot, way, 1, time).wait_send()
 
     loop(0, SLOTS, drain)
     loop(0, full, drain_z)
     loop(high, SLOTS, drain_z)
-    loop(0, full, lambda slot: drain_y(slot, every))
-    loop(full, high, lambda slot: drain_y(slot, own))
-    loop(0, full, drain_corner)
+    loop(0, full, lambda slot: drain_y(slot, (0, 1, 2), every))
+    loop(full, high, lambda slot: drain_y(slot, (0,), own))
     counts_swap().wait_send()
     for way in range(2):
         counts_z(way).wait_send()
@@ -446,8 +543,8 @@
         out_specs=(vmem, vmem, vmem),
         scratch_shapes=[
             pltpu.VMEM((SLOTS, 2, 2) + tile, BF16),
-            pltpu.VMEM((SLOTS, 2, 4, 3 * tokens, HD), BF16),
-            pltpu.VMEM((SLOTS, 2, 4, 3 * tokens, HD), BF16),
+            pltpu.VMEM((SLOTS, 2, 4, 3) + tile, BF16),
+            pltpu.VMEM((SLOTS, 2, 4, 3) + tile, BF16),
             pltpu.VMEM((2, SLOTS, 2, 4) + tile, BF16),
             pltpu.VMEM((2, SLOTS, 2) + tile, BF16),
             pltpu.VMEM((2, SLOTS, 2) + tile, BF16),
@@ -459,9 +556,8 @@
             pltpu.VMEM((3, 8, 128), jnp.int32),
             dma((2, SLOTS)), dma((2, SLOTS)),
             dma((2, SLOTS)), dma((2, SLOTS)),
-            dma((2, SLOTS)), dma((2, SLOTS)),
+            dma((3, 2, 2, SLOTS)), dma((3, 2, 2, SLOTS)),
             dma((2, 2, SLOTS)), dma((2, 2, SLOTS)),
-            dma((2, SLOTS)), dma((2, SLOTS)),
             dma((2, SLOTS)), dma((2, SLOTS)),
             dma((SLOTS,)), dma((SLOTS,)),
             dma((5,)), dma((5,)),
@@ -501,7 +597,21 @@
         perm, place, reach, frames_valid, rows_valid,
         flat(queries), flat(keys), flat(values), flat(grad_out),
     )
-    outs = tile_call(SLOTS, SLOTS, dims, 0, operands)
+    both = jnp.sum(time_reach * row_reach)
+    row_only = jnp.sum(row_reach) - both
+    time_only = jnp.sum(time_reach) - both
+    choice = jnp.int32(len(PLANS) - 1)
+    for index in reversed(range(len(PLANS) - 1)):
+        full, high = PLANS[index]
+        fits = (
+            (both <= 2 * full) & (both + row_only <= 2 * high) & (time_only <= 2 * (SLOTS - high))
+        )
+        choice = jnp.where(fits, index, choice)
+    branches = [
+        functools.partial(tile_call, full, high, dims, index)
+        for index, (full, high) in enumerate(PLANS)
+    ]
+    outs = lax.switch(choice, branches, operands) if len(branches) > 1 else branches[0](operands)
     return tuple(unflat(out) for out in outs)
 
 

time: 194 us -> 143 us (0.74)
  the two profiles are of different devices: /device:TPU:1 before, /device:TPU:9 now
where the time goes in v2:
time: 143 us
  Pallas kernels  130 us (91%)
  between operations  4.58 us (3%)
  loops' own time  4.19 us (3%)
  local copies, waits for them, and re-layouts  3.61 us (3%)
    pallas_call x1, Pallas kernels, tile_call(): pl.pallas_call(functools.partial(kernel, full, high, dims), out_shape=(ou...  130 us
    another operation x1, loops' own time, on_device(): lax.switch(choice, branches, operands)  4.19 us
    unnamed x5, local copies, waits for them, and re-layouts  2.96 us

profile of v2, /device:TPU:9, one launch (start us, length us, event | category | flops | bytes accessed | tf_op | source)
XLA Modules:
  0.0 143.2 jit_solution(15664686119401817379)
XLA Ops:
  0.6 0.0 copy-start
  0.6 0.7 copy-done
  1.3 0.7 add_bitcast_fusion
  5.9 0.2 convert_reduce_fusion
  6.1 0.1 select_reduce_fusion.1
  6.2 0.3 select_reduce_fusion
  6.5 134.4 %conditional.1 = ((bf16[144,1536]{1,0:T(8,128)(2,1)S(1)}, bf16[144,1536]{1,0:T(8,128)(2,1)S(1)}, bf16[144,1536]{1,0:T(8,128)(2,1)S(1)})) conditional(s32[]{:T(128)} %clamp.3, (s32[12]{0:T(128)S(1)}, s32[12]{0:T(128)S(1)}, s32[2,12]{0,1:T(8,128)S(1)}, s32[1]{0:T(128)}, s32[1]{0:T(128)}, /*index=5*/bf16[144,1536]{1,0:T(8,128)(2,1)}, ...), branch_computations={%region_6.7_spmd, %region_7.8_spmd, %region_8.9_spmd} | conditional | flops 3439853568 | bytes 3096776 | solution.py:614
  10.5 0.6 copy.12.radius
  11.1 129.6 %branch_2_fun.1 = (bf16[144,1536]{1,0:T(8,128)(2,1)S(1)}, bf16[144,1536]{1,0:T(8,128)(2,1)S(1)}, bf16[144,1536]{1,0:T(8,128)(2,1)S(1)}) custom-call(s32[12]{0:T(128)S(1)} %get-tuple-element.72.perm, s32[12]{0:T(128)S(1)} %get-tuple-element.73.place, s32[2,12]{1,0:T(2,128)} %copy.12.radius, s32[1]{0:T(128)} %get-tuple-element.75.fv, s32[1]{0:T(128)} %get-tuple-element.76.rv, ...), custom_call_target="tpu_custom_call" | custom-call | flops 3439853568 | bytes 3096576 | tf_op jit(solution)/shard_map/cond/branch_2_fun/pallas_call | solution.py:539
  140.9 0.8 copy.25
  141.7 0.8 copy.26
  142.5 0.8 copy.27
  (3 shorter events, 0.0 us)
Async XLA Ops:
  0.6 0.7 copy-start
